TPU v7x, 768 devices: a whole 4x8x12 slice. The times are simulated.
768 devices in a mesh: dp: 16 (over x, z_hi, core), fsdp: 48 (over y, z_lo).
Axes of the slice: x: 4, y: 8, z: 12 (z_hi: 2, z_lo: 6; z = z_hi * 6 + z_lo), core: 2. Of those that a mesh axis runs over, the one named last changes fastest.
Arguments:
- loader_rows: bfloat16 [16, 25344, 512], P('dp', 'fsdp'), may hold values from -6 to 6
- dest_list: int32 [16, 25344], P('dp', 'fsdp'), may hold values from 0 to 12287, as said below
- row_counts: int32 [16, 48], P('dp', 'fsdp'), may hold values from 0 to 528, as said below
- bucket_ids: int32 [16, 48], P('dp', 'fsdp'), may hold values from 0 to 2
- conv_weight: bfloat16 [4608, 256], P('fsdp'), may hold values from -0.09375 to 0.09375
- out_grad: bfloat16 [16, 12288, 256], P('dp', 'fsdp'), may hold values from -6 to 6
Outputs:
- section_out: bfloat16 [16, 12288, 256], P('dp', 'fsdp')
- input_grad: bfloat16 [16, 12288, 512], P('dp', 'fsdp')
- conv_grad: float32 [4608, 256], P('fsdp')
Inputs may be any that keep to these rules, and one draw needn't show every extreme that they name: `dest_list`: in each data group the used slots of all loader devices name each of the group's 12288 feature rows exactly once. From one loader device to the 256 rows of one device go at most 11 used slots, and every device receives exactly 11 from some loader device. Entries past a loader's count are arbitrary values in range. `row_counts`: the counts of a data group sum to 12288; in each data group some loader device uses all 528 slots.
All inputs are finite; a program needn't handle non-finite values.
Results may differ from a plain program's by a relative error of at most 0.0031.
Values may be sent and summed in bfloat16 or wider, within the bound.
A program may use at most 64 MiB of HBM per device.

v0:
```python
import functools

import jax
import jax.numpy as jnp
from jax import lax
from jax.experimental import pallas as pl
from jax.experimental.pallas import tpu as pltpu
from jax.sharding import PartitionSpec as P

GROUPS = 32
TAPS = 9
LANES = 128
MESH = pl.DeviceIdType.MESH
BF16 = jnp.bfloat16
F32 = jnp.float32
I32 = jnp.int32


def layout(mesh):
    dp, fsdp = mesh.shape["dp"], mesh.shape["fsdp"]
    across, height = (4, 2), 8
    if fsdp % height:
        height = 3
    if dp % 16:
        across = (4, 1)
    return across[0], across[1], height, fsdp // height


def dot(a, b, dims=((1,), (0,))):
    return lax.dot_general(a, b, (dims, ((), ())), preferred_element_type=F32)


def iota(shape, dim):
    return lax.broadcasted_iota(I32, shape, dim)


def group_total(row, size):
    width = row.shape[1]
    lane = iota(row.shape, 1)
    step = 1
    while step < size:
        up = pltpu.roll(row, width - step, 1)
        down = pltpu.roll(row, step, 1)
        row = row + jnp.where((lane & step) == 0, up, down)
        step *= 2
    return row


def column_sum(values):
    total = jnp.sum(values, axis=0, keepdims=True)
    return jnp.broadcast_to(total, (8, values.shape[1]))


def kernel(
    sizes,
    slots_ref, dest_ref, count_ref, bucket_ref, shard_ref, grad_ref,
    section_ref, igrad_ref, cgrad_ref,
    wide, send, recv, weight, shifts, gcols, xhat_ref, rstd_ref, hidden_ref, hidden_t, hgrad,
    wgrad, core_out, core_in, x_out, x_own, x_in, y_out, y_own, y_in, z_out, z_in, quarters,
    local_sem, a2a_s, a2a_r, wz_s, wz_r, wy_s, wy_r, wx_s, wx_r, wc_s, wc_r,
    gc_s, gc_r, gx_s, gx_r, gy_s, gy_r, gz_s, gz_r, gf_s, gf_r,
):
    X, H, Y, Z = sizes
    HZ = Z // 2
    peers = Y * Z
    load, channels = slots_ref.shape
    pixels, out_width = grad_ref.shape
    chunks = channels // LANES
    cap = load // peers
    block = (cap + 1) * chunks
    rows_w = weight.shape[2]
    dp = lax.axis_index("dp")
    me = lax.axis_index("fsdp")
    core = lax.rem(dp, 2)
    zh = lax.rem(lax.div(dp, 2), H)
    x = lax.div(dp, 2 * H)
    y = lax.div(me, Z)
    z = lax.rem(me, Z)
    active = lax.div(z, HZ) == core

    def dp_at(x_, zh_, core_):
        return (x_ * H + zh_) * 2 + core_

    def around(value, extent):
        return lax.rem(value + extent, extent)

    barrier = pltpu.get_barrier_semaphore()

    def greet(dp_, fsdp_):
        pl.semaphore_signal(barrier, inc=1, device_id=(dp_, fsdp_), device_id_type=MESH)

    def greet_plane(k, _):
        greet(dp, lax.rem(me + k, peers))
        return 0

    lax.fori_loop(1, peers, greet_plane, 0)
    for dx in range(1, X):
        for other in range(2):
            greet(dp_at(lax.rem(x + dx, X), zh, other), me)
    greet(dp_at(x, zh, 1 - core), me)
    for dh in range(1, H):
        for tz in range(Z):
            greet(dp_at(x, lax.rem(zh + dh, H), core), y * Z + tz)
    greeted = peers - 1 + 2 * (X - 1) + 1 + (H - 1) * Z

    dest = dest_ref[...]
    usable = iota(dest.shape, 1) < count_ref[...]
    owner = jnp.where(usable, lax.div(dest, pixels), -1)
    place = lax.rem(dest, pixels)
    owns = iota((peers, load), 0) == owner
    owns_f = jnp.where(owns, 1.0, 0.0)
    before = jnp.where(iota((load, load), 0) < iota((load, load), 1), 1.0, 0.0).astype(BF16)
    earlier = dot(owns_f.astype(BF16), before)
    rank = jnp.sum(owns_f * earlier, axis=0, keepdims=True).astype(I32)
    slot = jnp.where(usable, owner * (cap + 1) + rank, -1)
    rows_all = peers * (cap + 1)
    pick = jnp.where(iota((rows_all, load), 0) == slot, 1.0, 0.0).astype(BF16)
    packed = dot(pick, slots_ref[...])
    for c in range(chunks):
        wide[pl.ds(c, rows_all, stride=chunks), :] = packed[:, c * LANES : (c + 1) * LANES]
    marks = jnp.where(
        iota((LANES, load), 0) == rank, (place - pixels).astype(F32), 0.0
    ).astype(BF16)
    places = dot(owns_f.astype(BF16), marks, ((1,), (1,))) + float(pixels)
    wide[pl.ds(cap * chunks, peers, stride=block), :] = places
    send[...] = wide[...].astype(BF16).reshape(send.shape)

    pl.semaphore_wait(barrier, greeted)

    def remote(src, dst, s_sem, r_sem, where):
        return pltpu.make_async_remote_copy(
            src_ref=src, dst_ref=dst, send_sem=s_sem, recv_sem=r_sem, device_id=where, device_id_type=MESH
        )

    def lanes_of(x_):
        return pl.ds(pl.multiple_of(lax.rem(x_, 2) * LANES, LANES), LANES)

    def w_quarter(b, x_):
        return weight.at[b, lax.div(x_, 2), :, lanes_of(x_)]

    def w_chunk(y_, x_, core_):
        return weight.at[pl.ds(Z * y_ + HZ * core_, HZ), lax.div(x_, 2), :, lanes_of(x_)]

    shard_quarter = shard_ref.at[lax.div(x, 2), :, lanes_of(x)]

    def wz_copy(dz, target, b):
        return remote(shard_quarter, w_quarter(b, x), wz_s.at[dz], wz_r.at[dz], (dp, y * Z + target))

    def wy_copy(dy, y_src, y_dst):
        part = w_chunk(y_src, x, core)
        return remote(part, part, wy_s.at[dy], wy_r.at[dy], (dp, y_dst * Z + z))

    def wx_copy(dx, k, y_, x_src, x_dst):
        part = w_chunk(y_, x_src, core)
        return remote(part, part, wx_s.at[dx, k], wx_r.at[dx, k], (dp_at(x_dst, zh, core), me))

    def wc_copy(dx, k, y_, x_src, core_):
        part = w_chunk(y_, x_src, core_)
        return remote(part, part, wc_s.at[dx, k], wc_r.at[dx, k], (dp_at(x, zh, 1 - core), me))

    def a2a_copy(k, source, target):
        return remote(send.at[target], recv.at[source], a2a_s.at[k], a2a_r.at[k], (dp, target))

    def a2a_peer(k, sign):
        ty = around(y + sign * lax.div(k, Z), Y)
        tz = around(z + sign * lax.rem(k, Z), Z)
        return ty * Z + tz

    @pl.when(active)
    def _():
        own = pltpu.make_async_copy(shard_quarter, w_quarter(me, x), local_sem)
        own.start()
        for dz in range(1, Z):
            wz_copy(dz, around(z + dz, Z), me).start()
        own.wait()

    def a2a_start(k, _):
        a2a_copy(k, me, a2a_peer(k, 1)).start()
        return 0

    lax.fori_loop(1, peers, a2a_start, 0)
    recv[me] = send[me]

    bucket = bucket_ref[...]
    width = jnp.where(bucket == 0, 8, jnp.where(bucket == 1, 16, 32))
    grad = grad_ref[...]
    pixel = iota((pixels, pixels), 0)
    gap = iota((pixels, pixels), 1) - pixel
    column = pixel & (width - 1)

    def make_shift(t, _):
        a = lax.div(t, 3) - 1
        b = lax.rem(t, 3) - 1
        near = column + b
        hit = (gap == a * width + b) & (near >= 0) & (near < width)
        shift = jnp.where(hit, 1.0, 0.0).astype(BF16)
        shifts[t] = shift
        gcols[TAPS - 1 - t] = dot(shift, grad).astype(BF16)
        return 0

    lax.fori_loop(0, TAPS, make_shift, 0)

    for j in range(HZ):
        sz = HZ * core + j

        @pl.when(sz != z)
        def _(sz=sz):
            wz_copy(around(z - sz, Z), z, y * Z + sz).wait_recv()

    for dy in range(1, Y):
        wy_copy(dy, y, lax.rem(y + dy, Y)).start()

    def w_forward(k, _):
        sy = around(y - k, Y)

        @pl.when(k > 0)
        def _():
            wy_copy(k, sy, y).wait_recv()

        for dx in range(1, X):
            wx_copy(dx, k, sy, x, lax.rem(x + dx, X)).start()
        wc_copy(0, k, sy, x, core).start()
        return 0

    lax.fori_loop(0, Y, w_forward, 0)

    def w_cross(k, _):
        sy = around(y - k, Y)
        for dx in range(1, X):
            sx = around(x - dx, X)
            wx_copy(dx, k, sy, sx, x).wait_recv()
            wc_copy(dx, k, sy, sx, core).start()
        return 0

    lax.fori_loop(0, Y, w_cross, 0)

    def a2a_wait(k, _):
        a2a_copy(k, a2a_peer(k, -1), me).wait_recv()
        return 0

    lax.fori_loop(1, peers, a2a_wait, 0)
    wide[...] = recv[...].astype(F32).reshape(wide.shape)
    got_places = wide[pl.ds(cap * chunks, peers, stride=block), :].astype(BF16)
    index = iota((peers, rows_all), 1)
    spread = jnp.where(lax.div(index, cap + 1) == iota((peers, rows_all), 0), 1.0, 0.0).astype(BF16)
    by_rank = dot(got_places, spread, ((0,), (0,)))
    index = iota((LANES, rows_all), 1)
    fits = lax.rem(index, cap + 1) == iota((LANES, rows_all), 0)
    where_to = jnp.sum(jnp.where(fits, by_rank, 0.0), axis=0, keepdims=True).astype(I32)
    put = jnp.where(iota((pixels, rows_all), 0) == where_to, 1.0, 0.0).astype(BF16)
    features = jnp.concatenate(
        [dot(put, wide[pl.ds(c, rows_all, stride=chunks), :].astype(BF16)) for c in range(chunks)], axis=1
    )
    per_group = channels // GROUPS
    share = 1.0 / float(pixels * per_group)
    centre = group_total(column_sum(features), per_group) * share
    centred = features - centre[:1]
    spread_of = group_total(column_sum(centred * centred), per_group) * share
    rstd = lax.rsqrt(spread_of + 1e-05)
    xhat = centred * rstd[:1]
    hidden = xhat * jax.nn.sigmoid(xhat)
    rstd_ref[...] = rstd
    xhat_ref[...] = xhat
    hidden_t[...] = hidden.T.astype(BF16)
    hidden_ref[...] = hidden.astype(BF16)
    section_ref[...] = features[:, :out_width]

    def w_term(t, _):
        wgrad[pl.ds(pl.multiple_of(t * channels, channels), channels), :] = dot(hidden_t[...], gcols[t])
        return 0

    lax.fori_loop(0, TAPS, w_term, 0)

    rows_b = 2 * rows_w
    span = HZ * rows_b

    def my_rows(y_, core_):
        return pl.ds(pl.multiple_of((Z * y_ + HZ * core_) * rows_b, rows_b), span)

    def gc_copy(k, y_):
        return remote(core_out.at[y_], core_in.at[y_], gc_s.at[k], gc_r.at[k], (dp_at(x, zh, 1 - core), me))

    def gx_copy(dx, k, y_, x_):
        return remote(x_out.at[x_, y_], x_in.at[dx, y_], gx_s.at[dx, k], gx_r.at[dx, k], (dp_at(x_, zh, core), me))

    def gy_copy(k, y_):
        return remote(y_out.at[k], y_in.at[k], gy_s.at[k], gy_r.at[k], (dp, y_ * Z + z))

    def core_stage(k, _):
        y_ = lax.rem(y + k, Y)
        core_out[y_] = wgrad[my_rows(y_, 1 - core), :].astype(BF16).reshape(core_out.shape[1:])
        gc_copy(k, y_).start()
        return 0

    lax.fori_loop(0, Y, core_stage, 0)

    def x_stage(k, _):
        y_ = lax.rem(y + k, Y)
        gc_copy(k, y_).wait_recv()
        both = wgrad[my_rows(y_, core), :].reshape(core_in.shape[1:]) + core_in[y_].astype(F32)
        own = None
        for x_ in range(X):
            first = (x_ % 2) * LANES
            part = both[:, x_ // 2, :, first : first + LANES]
            x_out[x_, y_] = part.astype(BF16)
            own = part if own is None else jnp.where(x == x_, part, own)
        x_own[y_] = own
        for dx in range(1, X):
            gx_copy(dx, k, y_, lax.rem(x + dx, X)).start()
        return 0

    lax.fori_loop(0, Y, x_stage, 0)

    def w_last(k, _):
        sy = around(y - k, Y)
        for dx in range(X):
            wc_copy(dx, k, sy, around(x - dx, X), 1 - core).wait_recv()
        return 0

    lax.fori_loop(0, Y, w_last, 0)
    hgrad[...] = jnp.zeros_like(hgrad)
    taps_row = 3
    blocks_row = taps_row * channels // (2 * rows_w)

    def conv_row(i, _):
        kernel_row = weight[pl.ds(i * blocks_row, blocks_row)].reshape(taps_row * channels, out_width)
        for j in range(taps_row):
            t = i * taps_row + j
            tap = kernel_row[j * channels : (j + 1) * channels]
            hgrad[...] += dot(gcols[t], tap, ((1,), (1,)))
            near = dot(shifts[t], hidden_ref[...]).astype(BF16)
            section_ref[...] += dot(near, tap)
        return 0

    lax.fori_loop(0, TAPS // taps_row, conv_row, 0)
    xhat = xhat_ref[...]
    gate = jax.nn.sigmoid(xhat)
    slope = hgrad[...] * (gate * (1.0 + xhat * (1.0 - gate)))
    mean_s = group_total(column_sum(slope), per_group) * share
    mean_sx = group_total(column_sum(slope * xhat), per_group) * share
    back = rstd_ref[:1, :] * (slope - mean_s[:1] - xhat * mean_sx[:1])
    igrad_ref[:, :out_width] = (back[:, :out_width] + grad_ref[...].astype(F32)).astype(BF16)
    igrad_ref[:, out_width:] = back[:, out_width:].astype(BF16)

    def y_stage(k, _):
        y_ = lax.rem(y + k, Y)
        total = x_own[y_]
        for dx in range(1, X):
            gx_copy(dx, k, y_, x).wait_recv()
            total = total + x_in[dx, y_].astype(F32)

        y_own[...] = total
        y_out[k] = total.astype(BF16)
        gy_copy(k, y_).start()
        return 0

    lax.fori_loop(1, Y, y_stage, 0)
    total = x_own[y]
    for dx in range(1, X):
        gx_copy(dx, 0, y, x).wait_recv()
        total = total + x_in[dx, y].astype(F32)
    y_own[...] = total

    def y_add(k, _):
        gy_copy(k, y).wait_recv()
        y_own[...] += y_in[k].astype(F32)
        return 0

    lax.fori_loop(1, Y, y_add, 0)
    z_out[...] = y_own[...]

    def gz_copy(j, h_, sh, sz):
        return remote(z_out.at[j], z_in.at[sh, sz], gz_s.at[j, h_], gz_r.at[sh, sz], (dp_at(x, h_, core), y * Z + HZ * core + j))

    for j in range(HZ):
        for h_ in range(H):
            mine = (HZ * core + j == z) & (zh == h_)

            @pl.when(mine)
            def _(j=j):
                z_in[zh, z] = z_out[j]

            @pl.when(jnp.logical_not(mine))
            def _(j=j, h_=h_):
                gz_copy(j, h_, zh, z).start()

    def gf_copy(dx, core_, x_src, x_dst):
        return remote(quarters.at[x_src], quarters.at[x_src], gf_s.at[dx, core_], gf_r.at[x_src], (dp_at(x_dst, zh, core_), me))

    images = peers * dp_count(sizes)
    scale = 1.0 / float(images * pixels) ** 0.5

    @pl.when(active)
    def _():
        for h_ in range(H):
            for sz in range(Z):

                @pl.when(jnp.logical_not((zh == h_) & (z == sz)))
                def _(h_=h_, sz=sz):
                    gz_copy(0, 0, h_, sz).wait_recv()

        total = z_in[0, 0]
        for h_ in range(H):
            for sz in range(Z):
                if h_ or sz:
                    total = total + z_in[h_, sz]
        quarters[x] = total * scale
        gf_copy(0, 1 - core, x, x).start()
        for dx in range(1, X):
            for other in range(2):
                gf_copy(dx, other, x, lax.rem(x + dx, X)).start()

    for x_ in range(X):

        @pl.when(jnp.logical_not(active & (x == x_)))
        def _(x_=x_):
            gf_copy(0, 0, x_, x).wait_recv()

    for x_ in range(X):
        first = (x_ % 2) * LANES
        cgrad_ref[x_ // 2, :, first : first + LANES] = quarters[x_]

    def a2a_left(k, _):
        a2a_copy(k, me, a2a_peer(k, 1)).wait_send()
        return 0

    lax.fori_loop(1, peers, a2a_left, 0)

    @pl.when(active)
    def _():
        for dz in range(1, Z):
            wz_copy(dz, around(z + dz, Z), me).wait_send()
        gf_copy(0, 1 - core, x, x).wait_send()
        for dx in range(1, X):
            for other in range(2):
                gf_copy(dx, other, x, lax.rem(x + dx, X)).wait_send()

    for j in range(HZ):
        for h_ in range(H):

            @pl.when(jnp.logical_not((HZ * core + j == z) & (zh == h_)))
            def _(j=j, h_=h_):
                gz_copy(j, h_, zh, z).wait_send()

    for dy in range(1, Y):
        wy_copy(dy, y, lax.rem(y + dy, Y)).wait_send()
        gy_copy(dy, lax.rem(y + dy, Y)).wait_send()

    def rest_left(k, _):
        y_ = lax.rem(y + k, Y)
        sy = around(y - k, Y)
        gc_copy(k, y_).wait_send()
        wc_copy(0, k, sy, x, core).wait_send()
        for dx in range(1, X):
            wc_copy(dx, k, sy, around(x - dx, X), core).wait_send()
            wx_copy(dx, k, sy, x, lax.rem(x + dx, X)).wait_send()
            gx_copy(dx, k, y_, lax.rem(x + dx, X)).wait_send()
        return 0

    lax.fori_loop(0, Y, rest_left, 0)


def dp_count(sizes):
    return sizes[0] * sizes[1] * 2


def on_device(sizes, loader_rows, dest_list, row_counts, bucket_ids, conv_weight, out_grad):
    X, H, Y, Z = sizes
    HZ = Z // 2
    peers = Y * Z
    load, channels = loader_rows.shape[1:]
    pixels, out_width = out_grad.shape[1:]
    chunks = channels // LANES
    block = (load // peers + 1) * chunks
    rows_w = conv_weight.shape[0] // 2
    vmem = pltpu.VMEM
    sem = pltpu.SemaphoreType.DMA
    part = (HZ, rows_w, LANES)
    scratch = [
        vmem((peers * block, LANES), F32),
        vmem((peers, block, LANES), BF16),
        vmem((peers, block, LANES), BF16),
        vmem((peers, 2, rows_w, out_width), BF16),
        vmem((TAPS, pixels, pixels), BF16),
        vmem((TAPS, pixels, out_width), BF16),
        vmem((pixels, channels), F32),
        vmem((8, channels), F32),
        vmem((pixels, channels), BF16),
        vmem((channels, pixels), BF16),
        vmem((pixels, channels), F32),
        vmem((TAPS * channels, out_width), F32),
        vmem((Y, HZ, 2, rows_w, out_width), BF16),
        vmem((Y, HZ, 2, rows_w, out_width), BF16),
        vmem((X, Y, *part), BF16),
        vmem((Y, *part), F32),
        vmem((X, Y, *part), BF16),
        vmem((Y, *part), BF16),
        vmem(part, F32),
        vmem((Y, *part), BF16),
        vmem(part, F32),
        vmem((H, Z, rows_w, LANES), F32),
        vmem((X, rows_w, LANES), F32),
        sem,
        sem((peers,)), sem((peers,)),
        sem((Z,)), sem((Z,)),
        sem((Y,)), sem((Y,)),
        sem((X, Y)), sem((X, Y)),
        sem((X, Y)), sem((X, Y)),
        sem((Y,)), sem((Y,)),
        sem((X, Y)), sem((X, Y)),
        sem((Y,)), sem((Y,)),
        sem((HZ, H)), sem((H, Z)),
        sem((X, 2)), sem((X,)),
    ]
    whole = pl.BlockSpec(memory_space=pltpu.VMEM)
    flops = 2 * pixels * out_width * channels * TAPS * 3
    section, igrad, cgrad = pl.pallas_call(
        functools.partial(kernel, sizes),
        out_shape=(
            jax.ShapeDtypeStruct((pixels, out_width), F32),
            jax.ShapeDtypeStruct((pixels, channels), BF16),
            jax.ShapeDtypeStruct((2, rows_w, out_width), F32),
        ),
        in_specs=[whole] * 6,
        out_specs=(whole,) * 3,
        scratch_shapes=scratch,
        compiler_params=pltpu.CompilerParams(
            collective_id=0, has_side_effects=True, vmem_limit_bytes=48 * 2**20
        ),
        cost_estimate=pl.CostEstimate(flops=flops, bytes_accessed=2**21, transcendentals=0),
        name="residual_section",
    )(
        loader_rows[0],
        dest_list,
        row_counts,
        bucket_ids,
        conv_weight.reshape(2, rows_w, out_width),
        out_grad[0],
    )
    return section.astype(BF16)[None], igrad[None], cgrad.reshape(conv_weight.shape)


def solution(mesh):
    sizes = layout(mesh)
    in_specs = (
        P("dp", "fsdp", None),
        P("dp", "fsdp"),
        P("dp", "fsdp"),
        P("dp", "fsdp"),
        P("fsdp", None),
        P("dp", "fsdp", None),
    )
    out_specs = (P("dp", "fsdp", None), P("dp", "fsdp", None), P("fsdp", None))
    return jax.shard_map(
        functools.partial(on_device, sizes), mesh=mesh, in_specs=in_specs, out_specs=out_specs, check_vma=False
    )
```

profile of v0, /device:TPU:1, one launch (start us, length us, event | category | flops | bytes accessed | tf_op | source)
XLA Modules:
  0.0 99.8 jit_solution(3811669478440676804)
XLA Ops:
  1.9 0.0 copy-start.3
  1.9 0.7 copy-done.3
  2.6 0.0 copy-start
  2.6 1.0 %copy-done = bf16[1,528,512]{2,1,0:T(8,128)(2,1)S(1)} copy-done((bf16[1,528,512]{2,1,0:T(8,128)(2,1)S(1)}, bf16[1,528,512]{2,1,0:T(8,128)(2,1)}, u32[]{:S(2)}) %copy-start) | copy-done | bytes 540696
  3.7 0.0 copy-start.1
  3.7 0.9 copy-done.1
  4.6 0.0 copy-start.2
  4.6 0.8 copy-done.2
  5.4 92.5 %residual_section.1 = (f32[256,256]{1,0:T(8,128)S(1)}, bf16[256,512]{1,0:T(8,128)(2,1)S(1)}, f32[2,48,256]{2,1,0:T(8,128)S(1)}) custom-call(bf16[528,512]{1,0:T(8,128)(2,1)S(1)} %bitcast.9, s32[1,528]{1,0:T(1,128)S(1)} %copy-done.3, s32[1,1]{1,0:T(1,128)S(6)} %copy.11.count_ref, s32[1,1]{1,0:T(1,128)S(6)} %copy.12.bucket_ref, ...), custom_call_target="tpu_custom_call" | custom-call | flops 1811939328 | bytes 2097152 | tf_op jit(solution)/shard_map/residual_section/pallas_call | solution.py:517
  97.8 0.7 convert_bitcast_fusion
  98.5 0.7 copy.13
  99.2 0.6 copy.14
Async XLA Ops:
  1.9 0.7 copy-start.3
  2.6 1.0 %copy-start = (bf16[1,528,512]{2,1,0:T(8,128)(2,1)S(1)}, bf16[1,528,512]{2,1,0:T(8,128)(2,1)}, u32[]{:S(2)}) copy-start(bf16[1,528,512]{2,1,0:T(8,128)(2,1)} %param.6) | copy-start | bytes 1622020
  3.7 0.9 copy-start.1
  4.6 0.8 copy-start.2
where the time goes:
time: 100 us; the launch traced here: 99.8 us
  Pallas kernels  92.5 us (92%)
  local copies, waits for them, and re-layouts  4.77 us (5%)
  between operations  1.94 us (2%)
    pallas_call x1, Pallas kernels, on_device(): pl.pallas_call(functools.partial(kernel, sizes), out_shape=(jax.ShapeDtyp...  92.5 us
    unnamed x10, local copies, waits for them, and re-layouts  4.77 us

commit v1 on v0

--- a/solution.py
+++ b/solution.py
@@ -53,11 +53,12 @@
 
 def kernel(
     sizes,
-    slots_ref, dest_ref, count_ref, bucket_ref, shard_ref, grad_ref,
-    section_ref, igrad_ref, cgrad_ref,
+    slots_hbm, dest_hbm, count_hbm, bucket_hbm, shard_ref, grad_hbm,
+    section_hbm, igrad_hbm, cgrad_hbm,
+    slots_ref, dest_ref, count_ref, bucket_ref, grad_ref, section_ref, section_out, igrad_ref, cgrad_ref,
     wide, send, recv, weight, shifts, gcols, xhat_ref, rstd_ref, hidden_ref, hidden_t, hgrad,
     wgrad, core_out, core_in, x_out, x_own, x_in, y_out, y_own, y_in, z_out, z_in, quarters,
-    local_sem, a2a_s, a2a_r, wz_s, wz_r, wy_s, wy_r, wx_s, wx_r, wc_s, wc_r,
+    in_sem, out_sem, local_sem, a2a_s, a2a_r, wz_s, wz_r, wy_s, wy_r, wx_s, wx_r, wc_s, wc_r,
     gc_s, gc_r, gx_s, gx_r, gy_s, gy_r, gz_s, gz_r, gf_s, gf_r,
 ):
     X, H, Y, Z = sizes
@@ -84,6 +85,27 @@
     def around(value, extent):
         return lax.rem(value + extent, extent)
 
+    arriving = [
+        pltpu.make_async_copy(src, dst, in_sem.at[n])
+        for n, (src, dst) in enumerate(
+            (
+                (dest_hbm, dest_ref),
+                (count_hbm, count_ref),
+                (slots_hbm, slots_ref),
+                (bucket_hbm, bucket_ref),
+                (grad_hbm, grad_ref),
+            )
+        )
+    ]
+    for copy in arriving:
+        copy.start()
+    lanes = pl.ds(pl.multiple_of(lax.rem(x, 2) * LANES, LANES), LANES)
+    own_piece = pltpu.make_async_copy(shard_ref.at[lax.div(x, 2), :, lanes], weight.at[x, me], local_sem)
+
+    @pl.when(active)
+    def _():
+        own_piece.start()
+
     barrier = pltpu.get_barrier_semaphore()
 
     def greet(dp_, fsdp_):
@@ -103,6 +125,8 @@
             greet(dp_at(x, lax.rem(zh + dh, H), core), y * Z + tz)
     greeted = peers - 1 + 2 * (X - 1) + 1 + (H - 1) * Z
 
+    for copy in arriving:
+        copy.wait()
     dest = dest_ref[...]
     usable = iota(dest.shape, 1) < count_ref[...]
     owner = jnp.where(usable, lax.div(dest, pixels), -1)
@@ -132,23 +156,19 @@
             src_ref=src, dst_ref=dst, send_sem=s_sem, recv_sem=r_sem, device_id=where, device_id_type=MESH
         )
 
-    def lanes_of(x_):
-        return pl.ds(pl.multiple_of(lax.rem(x_, 2) * LANES, LANES), LANES)
-
     def w_quarter(b, x_):
-        return weight.at[b, lax.div(x_, 2), :, lanes_of(x_)]
+        return weight.at[x_, b]
 
     def w_chunk(y_, x_, core_):
-        return weight.at[pl.ds(Z * y_ + HZ * core_, HZ), lax.div(x_, 2), :, lanes_of(x_)]
-
-    shard_quarter = shard_ref.at[lax.div(x, 2), :, lanes_of(x)]
+        return weight.at[x_, pl.ds(Z * y_ + HZ * core_, HZ)]
 
     def wz_copy(dz, target, b):
-        return remote(shard_quarter, w_quarter(b, x), wz_s.at[dz], wz_r.at[dz], (dp, y * Z + target))
-
-    def wy_copy(dy, y_src, y_dst):
+        part = w_quarter(b, x)
+        return remote(part, part, wz_s.at[dz], wz_r.at[dz], (dp, y * Z + target))
+
+    def wy_copy(k, y_src, y_dst):
         part = w_chunk(y_src, x, core)
-        return remote(part, part, wy_s.at[dy], wy_r.at[dy], (dp, y_dst * Z + z))
+        return remote(part, part, wy_s.at[k], wy_r.at[k], (dp, y_dst * Z + z))
 
     def wx_copy(dx, k, y_, x_src, x_dst):
         part = w_chunk(y_, x_src, core)
@@ -168,11 +188,9 @@
 
     @pl.when(active)
     def _():
-        own = pltpu.make_async_copy(shard_quarter, w_quarter(me, x), local_sem)
-        own.start()
+        own_piece.wait()
         for dz in range(1, Z):
             wz_copy(dz, around(z + dz, Z), me).start()
-        own.wait()
 
     def a2a_start(k, _):
         a2a_copy(k, me, a2a_peer(k, 1)).start()
@@ -198,7 +216,7 @@
         gcols[TAPS - 1 - t] = dot(shift, grad).astype(BF16)
         return 0
 
-    lax.fori_loop(0, TAPS, make_shift, 0)
+    lax.fori_loop(0, TAPS, make_shift, 0, unroll=3)
 
     for j in range(HZ):
         sz = HZ * core + j
@@ -223,16 +241,6 @@
         return 0
 
     lax.fori_loop(0, Y, w_forward, 0)
-
-    def w_cross(k, _):
-        sy = around(y - k, Y)
-        for dx in range(1, X):
-            sx = around(x - dx, X)
-            wx_copy(dx, k, sy, sx, x).wait_recv()
-            wc_copy(dx, k, sy, sx, core).start()
-        return 0
-
-    lax.fori_loop(0, Y, w_cross, 0)
 
     def a2a_wait(k, _):
         a2a_copy(k, a2a_peer(k, -1), me).wait_recv()
@@ -269,7 +277,7 @@
         wgrad[pl.ds(pl.multiple_of(t * channels, channels), channels), :] = dot(hidden_t[...], gcols[t])
         return 0
 
-    lax.fori_loop(0, TAPS, w_term, 0)
+    lax.fori_loop(0, TAPS, w_term, 0, unroll=True)
 
     rows_b = 2 * rows_w
     span = HZ * rows_b
@@ -311,6 +319,32 @@
 
     lax.fori_loop(0, Y, x_stage, 0)
 
+    def w_cross(k, _):
+        sy = around(y - k, Y)
+        for dx in range(1, X):
+            sx = around(x - dx, X)
+            wx_copy(dx, k, sy, sx, x).wait_recv()
+            wc_copy(dx, k, sy, sx, core).start()
+        return 0
+
+    lax.fori_loop(0, Y, w_cross, 0)
+
+    def x_total(k, y_):
+        total = x_own[y_]
+        for dx in range(1, X):
+            gx_copy(dx, k, y_, x).wait_recv()
+            total = total + x_in[dx, y_].astype(F32)
+        return total
+
+    def y_stage(k, _):
+        y_ = lax.rem(y + k, Y)
+        y_out[k] = x_total(k, y_).astype(BF16)
+        gy_copy(k, y_).start()
+        return 0
+
+    lax.fori_loop(1, Y, y_stage, 0)
+    y_own[...] = x_total(0, y)
+
     def w_last(k, _):
         sy = around(y - k, Y)
         for dx in range(X):
@@ -323,7 +357,12 @@
     blocks_row = taps_row * channels // (2 * rows_w)
 
     def conv_row(i, _):
-        kernel_row = weight[pl.ds(i * blocks_row, blocks_row)].reshape(taps_row * channels, out_width)
+        blocks = pl.ds(i * blocks_row, blocks_row)
+        halves = [
+            jnp.stack([weight[2 * r + h, blocks] for r in range(2)], axis=1).reshape(taps_row * channels, LANES)
+            for h in range(2)
+        ]
+        kernel_row = jnp.concatenate(halves, axis=1)
         for j in range(taps_row):
             t = i * taps_row + j
             tap = kernel_row[j * channels : (j + 1) * channels]
@@ -333,6 +372,7 @@
         return 0
 
     lax.fori_loop(0, TAPS // taps_row, conv_row, 0)
+    section_out[...] = section_ref[...].astype(BF16)
     xhat = xhat_ref[...]
     gate = jax.nn.sigmoid(xhat)
     slope = hgrad[...] * (gate * (1.0 + xhat * (1.0 - gate)))
@@ -341,25 +381,14 @@
     back = rstd_ref[:1, :] * (slope - mean_s[:1] - xhat * mean_sx[:1])
     igrad_ref[:, :out_width] = (back[:, :out_width] + grad_ref[...].astype(F32)).astype(BF16)
     igrad_ref[:, out_width:] = back[:, out_width:].astype(BF16)
-
-    def y_stage(k, _):
-        y_ = lax.rem(y + k, Y)
-        total = x_own[y_]
-        for dx in range(1, X):
-            gx_copy(dx, k, y_, x).wait_recv()
-            total = total + x_in[dx, y_].astype(F32)
-
-        y_own[...] = total
-        y_out[k] = total.astype(BF16)
-        gy_copy(k, y_).start()
-        return 0
-
-    lax.fori_loop(1, Y, y_stage, 0)
-    total = x_own[y]
-    for dx in range(1, X):
-        gx_copy(dx, 0, y, x).wait_recv()
-        total = total + x_in[dx, y].astype(F32)
-    y_own[...] = total
+    leaving = [
+        pltpu.make_async_copy(src, dst, out_sem.at[n])
+        for n, (src, dst) in enumerate(
+            ((section_out, section_hbm), (igrad_ref, igrad_hbm), (cgrad_ref, cgrad_hbm))
+        )
+    ]
+    leaving[0].start()
+    leaving[1].start()
 
     def y_add(k, _):
         gy_copy(k, y).wait_recv()
@@ -419,6 +448,7 @@
     for x_ in range(X):
         first = (x_ % 2) * LANES
         cgrad_ref[x_ // 2, :, first : first + LANES] = quarters[x_]
+    leaving[2].start()
 
     def a2a_left(k, _):
         a2a_copy(k, me, a2a_peer(k, 1)).wait_send()
@@ -441,10 +471,6 @@
             @pl.when(jnp.logical_not((HZ * core + j == z) & (zh == h_)))
             def _(j=j, h_=h_):
                 gz_copy(j, h_, zh, z).wait_send()
-
-    for dy in range(1, Y):
-        wy_copy(dy, y, lax.rem(y + dy, Y)).wait_send()
-        gy_copy(dy, lax.rem(y + dy, Y)).wait_send()
 
     def rest_left(k, _):
         y_ = lax.rem(y + k, Y)
@@ -458,6 +484,28 @@
         return 0
 
     lax.fori_loop(0, Y, rest_left, 0)
+
+    def y_left(k, _):
+        wy_copy(k, y, lax.rem(y + k, Y)).wait_send()
+        gy_copy(k, lax.rem(y + k, Y)).wait_send()
+        return 0
+
+    lax.fori_loop(1, Y, y_left, 0)
+    for copy in leaving:
+        copy.wait()
+
+
+def deliver(*refs):
+    sources, targets, held, sems = refs[:3], refs[3:6], refs[6:9], refs[9]
+    inward = [pltpu.make_async_copy(sources[n], held[n], sems.at[n]) for n in range(3)]
+    outward = [pltpu.make_async_copy(held[n], targets[n], sems.at[n + 3]) for n in range(3)]
+    for copy in inward:
+        copy.start()
+    for n in range(3):
+        inward[n].wait()
+        outward[n].start()
+    for copy in outward:
+        copy.wait()
 
 
 def dp_count(sizes):
@@ -477,10 +525,19 @@
     sem = pltpu.SemaphoreType.DMA
     part = (HZ, rows_w, LANES)
     scratch = [
+        vmem((load, channels), BF16),
+        vmem((1, load), I32),
+        vmem((1, 1), I32),
+        vmem((1, 1), I32),
+        vmem((pixels, out_width), BF16),
+        vmem((pixels, out_width), F32),
+        vmem((pixels, out_width), BF16),
+        vmem((pixels, channels), BF16),
+        vmem((2, rows_w, out_width), F32),
         vmem((peers * block, LANES), F32),
         vmem((peers, block, LANES), BF16),
         vmem((peers, block, LANES), BF16),
-        vmem((peers, 2, rows_w, out_width), BF16),
+        vmem((X, peers, rows_w, LANES), BF16),
         vmem((TAPS, pixels, pixels), BF16),
         vmem((TAPS, pixels, out_width), BF16),
         vmem((pixels, channels), F32),
@@ -500,7 +557,7 @@
         vmem(part, F32),
         vmem((H, Z, rows_w, LANES), F32),
         vmem((X, rows_w, LANES), F32),
-        sem,
+        sem((5,)), sem((3,)), sem,
         sem((peers,)), sem((peers,)),
         sem((Z,)), sem((Z,)),
         sem((Y,)), sem((Y,)),
@@ -512,20 +569,20 @@
         sem((HZ, H)), sem((H, Z)),
         sem((X, 2)), sem((X,)),
     ]
-    whole = pl.BlockSpec(memory_space=pltpu.VMEM)
+    anywhere = pl.BlockSpec(memory_space=pl.ANY)
     flops = 2 * pixels * out_width * channels * TAPS * 3
     section, igrad, cgrad = pl.pallas_call(
         functools.partial(kernel, sizes),
         out_shape=(
-            jax.ShapeDtypeStruct((pixels, out_width), F32),
+            jax.ShapeDtypeStruct((pixels, out_width), BF16),
             jax.ShapeDtypeStruct((pixels, channels), BF16),
             jax.ShapeDtypeStruct((2, rows_w, out_width), F32),
         ),
-        in_specs=[whole] * 6,
-        out_specs=(whole,) * 3,
+        in_specs=[anywhere] * 6,
+        out_specs=(anywhere,) * 3,
         scratch_shapes=scratch,
         compiler_params=pltpu.CompilerParams(
-            collective_id=0, has_side_effects=True, vmem_limit_bytes=48 * 2**20
+            collective_id=0, has_side_effects=True, vmem_limit_bytes=60 * 2**20
         ),
         cost_estimate=pl.CostEstimate(flops=flops, bytes_accessed=2**21, transcendentals=0),
         name="residual_section",
@@ -537,7 +594,15 @@
         conv_weight.reshape(2, rows_w, out_width),
         out_grad[0],
     )
-    return section.astype(BF16)[None], igrad[None], cgrad.reshape(conv_weight.shape)
+    section, igrad, cgrad = pl.pallas_call(
+        deliver,
+        out_shape=tuple(jax.ShapeDtypeStruct(a.shape, a.dtype) for a in (section, igrad, cgrad)),
+        in_specs=[anywhere] * 3,
+        out_specs=(anywhere,) * 3,
+        scratch_shapes=[*(vmem(a.shape, a.dtype) for a in (section, igrad, cgrad)), sem((6,))],
+        name="deliver",
+    )(section, igrad, cgrad)
+    return section[None], igrad[None], cgrad.reshape(conv_weight.shape)
 
 
 def solution(mesh):

time: 100 us -> 88.4 us (0.88)
  Pallas kernels: 92.5 us -> 86.3 us
  local copies, waits for them, and re-layouts: 4.77 us -> 0 us
    pallas_call x1, Pallas kernels: 92.5 us -> 84.5 us  [on_device(): pl.pallas_call(functools.partial(kernel, sizes), out_shape=(jax.ShapeDtyp...]
    unnamed x10 -> x0, local copies, waits for them, and re-layouts: 4.77 us -> none
    pallas_call x0 -> x1, Pallas kernels: none -> 1.8 us  [on_device(): pl.pallas_call(deliver, out_shape=tuple((jax.ShapeDtypeStruct(a.shape, a....]
where the time goes in v1:
time: 88.4 us; the launch traced here: 88.2 us
  Pallas kernels  86.3 us (98%)
  between operations  1.93 us (2%)
    pallas_call x1, Pallas kernels, on_device(): pl.pallas_call(functools.partial(kernel, sizes), out_shape=(jax.ShapeDtyp...  84.5 us
    pallas_call x1, Pallas kernels, on_device(): pl.pallas_call(deliver, out_shape=tuple((jax.ShapeDtypeStruct(a.shape, a....  1.8 us

profile of v1, /device:TPU:1, one launch (start us, length us, event | category | flops | bytes accessed | tf_op | source)
XLA Modules:
  0.0 88.2 jit_solution(11816418922871942519)
XLA Ops:
  1.9 84.5 %residual_section.1 = (bf16[256,256]{1,0:T(8,128)(2,1)}, bf16[256,512]{1,0:T(8,128)(2,1)}, f32[2,48,256]{2,1,0:T(8,128)}) custom-call(bf16[528,512]{1,0:T(8,128)(2,1)} %bitcast.6, s32[1,528]{1,0:T(1,128)} %dest_hbm.1, s32[1,1]{1,0:T(1,128)S(6)} %copy.9.count_hbm, s32[1,1]{1,0:T(1,128)S(6)} %copy.10.bucket_hbm, bf16[2,48,256]{2,1,0:T(8,128)(2,1)} %bitcast.11, ...), custom_call_target="tpu_custom_call" | custom-call | flops 1811939328 | bytes 2097152 | tf_op jit(solution)/shard_map/residual_section/pallas_call | solution.py:574
  86.4 1.8 %deliver.1 = (bf16[256,256]{1,0:T(8,128)(2,1)}, bf16[256,512]{1,0:T(8,128)(2,1)}, f32[2,48,256]{2,1,0:T(8,128)}) custom-call(bf16[256,256]{1,0:T(8,128)(2,1)} %get-tuple-element.9.refs_0_, bf16[256,512]{1,0:T(8,128)(2,1)} %get-tuple-element.10.refs_1_, f32[2,48,256]{2,1,0:T(8,128)} %get-tuple-element.11.refs_2_), custom_call_target="tpu_custom_call" | custom-call | tf_op jit(solution)/shard_map/deliver/pallas_call | solution.py:597

commit v2 on v1

--- a/solution.py
+++ b/solution.py
@@ -294,7 +294,14 @@
     def gy_copy(k, y_):
         return remote(y_out.at[k], y_in.at[k], gy_s.at[k], gy_r.at[k], (dp, y_ * Z + z))
 
-    def core_stage(k, _):
+    def farthest_first(i):
+        odd = lax.rem(i, 2)
+        return Y // 2 + lax.div(i, 2) * (1 - odd) - lax.div(i + 1, 2) * odd
+
+    far_x = sorted(range(1, X), key=lambda dx: -min(dx, X - dx))
+
+    def core_stage(i, _):
+        k = farthest_first(i)
         y_ = lax.rem(y + k, Y)
         core_out[y_] = wgrad[my_rows(y_, 1 - core), :].astype(BF16).reshape(core_out.shape[1:])
         gc_copy(k, y_).start()
@@ -302,7 +309,8 @@
 
     lax.fori_loop(0, Y, core_stage, 0)
 
-    def x_stage(k, _):
+    def x_stage(i, _):
+        k = farthest_first(i)
         y_ = lax.rem(y + k, Y)
         gc_copy(k, y_).wait_recv()
         both = wgrad[my_rows(y_, core), :].reshape(core_in.shape[1:]) + core_in[y_].astype(F32)
@@ -313,7 +321,7 @@
             x_out[x_, y_] = part.astype(BF16)
             own = part if own is None else jnp.where(x == x_, part, own)
         x_own[y_] = own
-        for dx in range(1, X):
+        for dx in far_x:
             gx_copy(dx, k, y_, lax.rem(x + dx, X)).start()
         return 0
 
@@ -336,14 +344,23 @@
             total = total + x_in[dx, y_].astype(F32)
         return total
 
-    def y_stage(k, _):
+    def y_stage(i, _):
+        k = farthest_first(i)
         y_ = lax.rem(y + k, Y)
-        y_out[k] = x_total(k, y_).astype(BF16)
-        gy_copy(k, y_).start()
-        return 0
-
-    lax.fori_loop(1, Y, y_stage, 0)
-    y_own[...] = x_total(0, y)
+        total = x_total(k, y_)
+
+        @pl.when(k == 0)
+        def _():
+            y_own[...] = total
+
+        @pl.when(k > 0)
+        def _():
+            y_out[k] = total.astype(BF16)
+            gy_copy(k, y_).start()
+
+        return 0
+
+    lax.fori_loop(0, Y, y_stage, 0)
 
     def w_last(k, _):
         sy = around(y - k, Y)
@@ -398,12 +415,17 @@
     lax.fori_loop(1, Y, y_add, 0)
     z_out[...] = y_own[...]
 
-    def gz_copy(j, h_, sh, sz):
-        return remote(z_out.at[j], z_in.at[sh, sz], gz_s.at[j, h_], gz_r.at[sh, sz], (dp_at(x, h_, core), y * Z + HZ * core + j))
-
-    for j in range(HZ):
-        for h_ in range(H):
-            mine = (HZ * core + j == z) & (zh == h_)
+    def gz_copy(j, dh, h_, sh, sz):
+        where = (dp_at(x, h_, core), y * Z + HZ * core + j)
+        return remote(z_out.at[j], z_in.at[sh, sz], gz_s.at[j, dh], gz_r.at[sh, sz], where)
+
+    for dh in (*range(1, H), 0):
+        h_ = lax.rem(zh + dh, H)
+        for j in range(HZ):
+            if dh:
+                gz_copy(j, dh, h_, zh, z).start()
+                continue
+            mine = HZ * core + j == z
 
             @pl.when(mine)
             def _(j=j):
@@ -411,7 +433,7 @@
 
             @pl.when(jnp.logical_not(mine))
             def _(j=j, h_=h_):
-                gz_copy(j, h_, zh, z).start()
+                gz_copy(j, 0, h_, zh, z).start()
 
     def gf_copy(dx, core_, x_src, x_dst):
         return remote(quarters.at[x_src], quarters.at[x_src], gf_s.at[dx, core_], gf_r.at[x_src], (dp_at(x_dst, zh, core_), me))
@@ -426,7 +448,7 @@
 
                 @pl.when(jnp.logical_not((zh == h_) & (z == sz)))
                 def _(h_=h_, sz=sz):
-                    gz_copy(0, 0, h_, sz).wait_recv()
+                    gz_copy(0, 0, zh, h_, sz).wait_recv()
 
         total = z_in[0, 0]
         for h_ in range(H):
@@ -434,10 +456,10 @@
                 if h_ or sz:
                     total = total + z_in[h_, sz]
         quarters[x] = total * scale
-        gf_copy(0, 1 - core, x, x).start()
-        for dx in range(1, X):
+        for dx in far_x:
             for other in range(2):
                 gf_copy(dx, other, x, lax.rem(x + dx, X)).start()
+        gf_copy(0, 1 - core, x, x).start()
 
     for x_ in range(X):
 
@@ -466,11 +488,12 @@
                 gf_copy(dx, other, x, lax.rem(x + dx, X)).wait_send()
 
     for j in range(HZ):
-        for h_ in range(H):
-
-            @pl.when(jnp.logical_not((HZ * core + j == z) & (zh == h_)))
-            def _(j=j, h_=h_):
-                gz_copy(j, h_, zh, z).wait_send()
+        for dh in range(1, H):
+            gz_copy(j, dh, lax.rem(zh + dh, H), zh, z).wait_send()
+
+        @pl.when(HZ * core + j != z)
+        def _(j=j):
+            gz_copy(j, 0, zh, zh, z).wait_send()
 
     def rest_left(k, _):
         y_ = lax.rem(y + k, Y)

time: 88.4 us -> 87.5 us (0.990)
  Pallas kernels: 86.3 us -> 85.4 us
    pallas_call x1, Pallas kernels: 84.5 us -> 83.6 us  [on_device(): pl.pallas_call(functools.partial(kernel, sizes), out_shape=(jax.ShapeDtyp...]
where the time goes in v2:
time: 87.5 us; the launch traced here: 87.3 us
  Pallas kernels  85.4 us (98%)
  between operations  1.93 us (2%)
    pallas_call x1, Pallas kernels, on_device(): pl.pallas_call(functools.partial(kernel, sizes), out_shape=(jax.ShapeDtyp...  83.6 us
    pallas_call x1, Pallas kernels, on_device(): pl.pallas_call(deliver, out_shape=tuple((jax.ShapeDtypeStruct(a.shape, a....  1.8 us

profile of v2, /device:TPU:1, one launch (start us, length us, event | category | flops | bytes accessed | tf_op | source)
XLA Modules:
  0.0 87.3 jit_solution(11261358642578805403)
XLA Ops:
  1.9 83.6 %residual_section.1 = (bf16[256,256]{1,0:T(8,128)(2,1)}, bf16[256,512]{1,0:T(8,128)(2,1)}, f32[2,48,256]{2,1,0:T(8,128)}) custom-call(bf16[528,512]{1,0:T(8,128)(2,1)} %bitcast.6, s32[1,528]{1,0:T(1,128)} %dest_hbm.1, s32[1,1]{1,0:T(1,128)S(6)} %copy.9.count_hbm, s32[1,1]{1,0:T(1,128)S(6)} %copy.10.bucket_hbm, bf16[2,48,256]{2,1,0:T(8,128)(2,1)} %bitcast.11, ...), custom_call_target="tpu_custom_call" | custom-call | flops 1811939328 | bytes 2097152 | tf_op jit(solution)/shard_map/residual_section/pallas_call | solution.py:597
  85.5 1.8 %deliver.1 = (bf16[256,256]{1,0:T(8,128)(2,1)}, bf16[256,512]{1,0:T(8,128)(2,1)}, f32[2,48,256]{2,1,0:T(8,128)}) custom-call(bf16[256,256]{1,0:T(8,128)(2,1)} %get-tuple-element.9.refs_0_, bf16[256,512]{1,0:T(8,128)(2,1)} %get-tuple-element.10.refs_1_, f32[2,48,256]{2,1,0:T(8,128)} %get-tuple-element.11.refs_2_), custom_call_target="tpu_custom_call" | custom-call | tf_op jit(solution)/shard_map/deliver/pallas_call | solution.py:620

commit v3 on v2

--- a/solution.py
+++ b/solution.py
@@ -273,12 +273,6 @@
     hidden_ref[...] = hidden.astype(BF16)
     section_ref[...] = features[:, :out_width]
 
-    def w_term(t, _):
-        wgrad[pl.ds(pl.multiple_of(t * channels, channels), channels), :] = dot(hidden_t[...], gcols[t])
-        return 0
-
-    lax.fori_loop(0, TAPS, w_term, 0, unroll=True)
-
     rows_b = 2 * rows_w
     span = HZ * rows_b
 
@@ -294,23 +288,35 @@
     def gy_copy(k, y_):
         return remote(y_out.at[k], y_in.at[k], gy_s.at[k], gy_r.at[k], (dp, y_ * Z + z))
 
-    def farthest_first(i):
-        odd = lax.rem(i, 2)
-        return Y // 2 + lax.div(i, 2) * (1 - odd) - lax.div(i + 1, 2) * odd
-
     far_x = sorted(range(1, X), key=lambda dx: -min(dx, X - dx))
 
+    rows_y = Z * rows_b
+    taps_y = -(-rows_y // channels)
+
+    def piece(i):
+        return lax.rem(i + 1, Y)
+
+    def w_term(t):
+        wgrad[pl.ds(pl.multiple_of(t * channels, channels), channels), :] = dot(hidden_t[...], gcols[t])
+
     def core_stage(i, _):
-        k = farthest_first(i)
+        k = piece(i)
         y_ = lax.rem(y + k, Y)
+        first = lax.div(y_ * rows_y, channels)
+        if rows_y % channels:
+            @pl.when((i == 0) | (y_ == 0))
+            def _():
+                w_term(first)
+        else:
+            w_term(first)
+        for later in range(1, taps_y):
+            w_term(first + later)
         core_out[y_] = wgrad[my_rows(y_, 1 - core), :].astype(BF16).reshape(core_out.shape[1:])
         gc_copy(k, y_).start()
         return 0
 
-    lax.fori_loop(0, Y, core_stage, 0)
-
     def x_stage(i, _):
-        k = farthest_first(i)
+        k = piece(i)
         y_ = lax.rem(y + k, Y)
         gc_copy(k, y_).wait_recv()
         both = wgrad[my_rows(y_, core), :].reshape(core_in.shape[1:]) + core_in[y_].astype(F32)
@@ -325,7 +331,15 @@
             gx_copy(dx, k, y_, lax.rem(x + dx, X)).start()
         return 0
 
-    lax.fori_loop(0, Y, x_stage, 0)
+    def both_stages(i, _):
+        core_stage(i + lag, 0)
+        x_stage(i, 0)
+        return 0
+
+    lag = 2
+    lax.fori_loop(0, lag, core_stage, 0)
+    lax.fori_loop(0, Y - lag, both_stages, 0)
+    lax.fori_loop(Y - lag, Y, x_stage, 0)
 
     def w_cross(k, _):
         sy = around(y - k, Y)
@@ -345,7 +359,7 @@
         return total
 
     def y_stage(i, _):
-        k = farthest_first(i)
+        k = piece(i)
         y_ = lax.rem(y + k, Y)
         total = x_total(k, y_)
 

time: 87.5 us -> 87.2 us (level)
  no operation moved by 1% of the time
where the time goes in v3:
time: 87.2 us; the launch traced here: 87.1 us
  Pallas kernels  85.1 us (98%)
  between operations  1.93 us (2%)
    pallas_call x1, Pallas kernels, on_device(): pl.pallas_call(functools.partial(kernel, sizes), out_shape=(jax.ShapeDtyp...  83.3 us
    pallas_call x1, Pallas kernels, on_device(): pl.pallas_call(deliver, out_shape=tuple((jax.ShapeDtypeStruct(a.shape, a....  1.8 us

profile of v3, /device:TPU:1, one launch (start us, length us, event | category | flops | bytes accessed | tf_op | source)
XLA Modules:
  0.0 87.1 jit_solution(2253383668586176712)
XLA Ops:
  1.9 83.3 %residual_section.1 = (bf16[256,256]{1,0:T(8,128)(2,1)}, bf16[256,512]{1,0:T(8,128)(2,1)}, f32[2,48,256]{2,1,0:T(8,128)}) custom-call(bf16[528,512]{1,0:T(8,128)(2,1)} %bitcast.6, s32[1,528]{1,0:T(1,128)} %dest_hbm.1, s32[1,1]{1,0:T(1,128)S(6)} %copy.9.count_hbm, s32[1,1]{1,0:T(1,128)S(6)} %copy.10.bucket_hbm, bf16[2,48,256]{2,1,0:T(8,128)(2,1)} %bitcast.11, ...), custom_call_target="tpu_custom_call" | custom-call | flops 1811939328 | bytes 2097152 | tf_op jit(solution)/shard_map/residual_section/pallas_call | solution.py:611
  85.3 1.8 %deliver.1 = (bf16[256,256]{1,0:T(8,128)(2,1)}, bf16[256,512]{1,0:T(8,128)(2,1)}, f32[2,48,256]{2,1,0:T(8,128)}) custom-call(bf16[256,256]{1,0:T(8,128)(2,1)} %get-tuple-element.9.refs_0_, bf16[256,512]{1,0:T(8,128)(2,1)} %get-tuple-element.10.refs_1_, f32[2,48,256]{2,1,0:T(8,128)} %get-tuple-element.11.refs_2_), custom_call_target="tpu_custom_call" | custom-call | tf_op jit(solution)/shard_map/deliver/pallas_call | solution.py:634
